TPU v7x, 256 devices: a whole 4x4x8 slice. The times are simulated.
256 devices in a mesh: depth: 64 (over x_hi, y, z), band: 4 (over x_lo, core).
Axes of the slice: x: 4 (x_hi: 2, x_lo: 2; x = x_hi * 2 + x_lo), y: 4, z: 8, core: 2. Of those that a mesh axis runs over, the one named last changes fastest.
Arguments:
- planes: float32 [64, 256, 2048], P('depth', 'band'), may hold values from -6 to 6
- denoised: float32 [64, 256, 2048], P('depth', 'band'), may hold values from -6 to 6
- scaled_dual: float32 [64, 256, 2048], P('depth', 'band'), may hold values from -4 to 4
- measured: float32 [256, 2048], P('band'), may hold values from -6 to 6
- lenslet_psf: bfloat16 [64, 31, 31], P('depth'), may hold values from -0.0234375 to 0.0234375
- kernel: bfloat16 [27, 16], replicated, may hold values from -1.25 to 1.25
- layer_bias: float32 [16], replicated, may hold values from -3 to 3
- mix_weight: bfloat16 [16], replicated, may hold values from -1.5 to 1.5
Outputs:
- new_planes: float32 [64, 256, 2048], P('depth', 'band')
- new_denoised: float32 [64, 256, 2048], P('depth', 'band')
- new_dual: float32 [64, 256, 2048], P('depth', 'band')
All inputs are finite; a program needn't handle non-finite values.
Results may differ from a plain program's by a relative error of at most 0.0049.
Values may be sent and summed in bfloat16 or wider, within the bound.
No kernel may reach another device: no remote copies, remote signals or barrier semaphores. Data moves between devices by JAX's collectives and lax.ppermute only.
A program may use at most 128 MiB of HBM per device.

v0:
```python
import jax
import jax.numpy as jnp
from jax import lax
from jax.sharding import PartitionSpec as P

KS = 31
step_size = 4.0
penalty = 0.5


def padded_2(block, sides, width):
    for axis, dim in sides:
        count = lax.axis_size(axis)
        forward = [(i, i + 1) for i in range(count - 1)]
        backward = [(target, source) for source, target in forward]
        low = lax.ppermute(
            lax.slice_in_dim(block, block.shape[dim] - width, None, axis=dim), axis, forward
        )
        high = lax.ppermute(lax.slice_in_dim(block, 0, width, axis=dim), axis, backward)
        block = jnp.concatenate([low, block, high], axis=dim)
    return block


def project(rimmed, psf_one):
    span_rows = rimmed.shape[0] - KS + 1
    total_cols = rimmed.shape[1]
    col_block = 256
    window_cols = col_block + KS - 1
    edge = KS // 2
    padded = jnp.pad(rimmed, ((0, 0), (edge, edge)))
    offsets = jnp.arange(window_cols)[:, None] - jnp.arange(col_block)[None, :]
    onehot = (offsets[None] == jnp.arange(KS)[:, None, None]).astype(jnp.bfloat16)
    band_matrix = jnp.einsum("ab,btj->atj", psf_one, onehot, preferred_element_type=jnp.float32)
    band_matrix = band_matrix.astype(jnp.bfloat16).reshape(KS * window_cols, col_block)
    pieces = []
    for b in range(total_cols // col_block):
        window = padded[:, b * col_block : b * col_block + window_cols]
        stacked = jnp.stack([window[a : a + span_rows] for a in range(KS)], axis=1)
        stacked = stacked.reshape(span_rows, KS * window_cols)
        pieces.append(jnp.dot(stacked, band_matrix, preferred_element_type=jnp.float32))
    return jnp.concatenate(pieces, axis=1)


def shards(planes, denoised, scaled_dual, measured, lenslet_psf, kernel, layer_bias, mix_weight):
    plane_count, band_rows, total_cols = planes.shape
    edge = KS // 2
    planes_half = planes.astype(jnp.bfloat16)
    rimmed = padded_2(planes_half, (("band", 1),), edge)
    partial_value = project(rimmed[0], lenslet_psf[0])
    sensor = lax.psum(partial_value, "depth")
    residual = (sensor - measured).astype(jnp.bfloat16)
    residual_rimmed = padded_2(residual, (("band", 0),), edge)
    gradient = jnp.stack([project(residual_rimmed, lenslet_psf[0][::-1, ::-1])])
    new_planes = planes - step_size * (gradient + penalty * (planes - (denoised - scaled_dual)))
    noisy = new_planes + scaled_dual
    noisy_half = noisy.astype(jnp.bfloat16)
    volume = padded_2(noisy_half, (("depth", 0), ("band", 1)), 1)
    volume = jnp.pad(volume, ((0, 0), (0, 0), (1, 1)))
    taps = []
    for i in range(3):
        for j in range(3):
            for k in range(3):
                taps.append(volume[i : i + plane_count, j : j + band_rows, k : k + total_cols])
    stacked = jnp.stack(taps)
    hidden = jnp.einsum("kn,kprc->nprc", kernel, stacked, preferred_element_type=jnp.float32)
    hidden = jnp.maximum(hidden + layer_bias[:, None, None, None], 0.0).astype(jnp.bfloat16)
    noise = jnp.einsum("n,nprc->prc", mix_weight, hidden, preferred_element_type=jnp.float32)
    new_denoised = noisy - noise
    new_dual = scaled_dual + new_planes - new_denoised
    return (new_planes, new_denoised, new_dual)


def solution(mesh):
    in_specs = (
        P("depth", "band", None),
        P("depth", "band", None),
        P("depth", "band", None),
        P("band", None),
        P("depth", None, None),
        P(),
        P(),
        P(),
    )
    out_specs = (P("depth", "band", None), P("depth", "band", None), P("depth", "band", None))
    return jax.shard_map(shards, mesh=mesh, in_specs=in_specs, out_specs=out_specs, check_vma=False)
```

profile of v0, /device:TPU:5, one launch (start us, length us, event | category | flops | bytes accessed | tf_op | source)
XLA Modules:
  0.0 905.9 jit_solution(1731038789126102001)
XLA Ops:
  8.3 3.4 collective-permute-start
  11.7 1.9 collective-permute-start.1
  13.7 2.9 convert_bitcast_fusion.1
  19.3 1.2 constant_dynamic-update-slice_fusion.152
  20.5 1.2 constant_dynamic-update-slice_fusion.151
  21.6 1.2 constant_dynamic-update-slice_fusion.150
  22.8 1.2 constant_dynamic-update-slice_fusion.149
  24.0 1.2 constant_dynamic-update-slice_fusion.148
  25.1 1.2 constant_dynamic-update-slice_fusion.147
  27.4 1.2 constant_dynamic-update-slice_fusion.145
  28.6 1.2 constant_dynamic-update-slice_fusion.144
  29.7 1.2 constant_dynamic-update-slice_fusion.143
  30.9 1.2 constant_dynamic-update-slice_fusion.142
  32.1 1.2 constant_dynamic-update-slice_fusion.141
  33.2 1.2 constant_dynamic-update-slice_fusion.140
  39.0 1.2 constant_dynamic-update-slice_fusion.135
  43.7 1.2 constant_dynamic-update-slice_fusion.131
  55.7 5.2 fusion.30
  61.0 5.1 fusion.29
  66.0 5.3 fusion.28
  71.3 5.1 fusion.27
  76.3 5.5 fusion.26
  81.9 5.1 fusion.25
  86.9 5.1 fusion.24
  92.0 5.7 fusion.23
  98.6 645.6 %all-reduce.5.cloned.1.call-done = f32[64,2048]{1,0:T(8,128)} async-done(((f32[64,2048]{1,0:T(8,128)}), f32[64,2048]{1,0:T(8,128)}) %all-reduce.5.cloned.1.call-update) | async-done | bytes 524304 | tf_op jit(solution)/shard_map/psum | solution.py:50
  745.4 49.2 %collective-permute-start.2 = (bf16[15,2048]{1,0:T(8,128)(2,1)S(1)}, bf16[15,2048]{1,0:T(8,128)(2,1)S(1)}, u32[]{:S(2)}, u32[]{:S(2)}) collective-permute-start(bf16[15,2048]{1,0:T(8,128)(2,1)S(1)} %get-tuple-element.349), channel_id=1, source_target_pairs={{0,1},{1,2},{2,3},{4,5},{5,6},{6,7},{8,9},{9,10},{10,11},{12,13},{... | collective-permute-start | bytes 184328 | tf_op jit(solution)/shard_map/ppermute | solution.py:16
  794.6 2.2 convert_bitcast_fusion
  796.8 1.9 collective-permute-start.3
  800.5 1.9 collective-permute-done.3
  812.7 5.5 fusion.22
  823.6 5.0 fusion.21
  828.6 5.2 fusion.20
  833.8 5.1 fusion.19
  838.9 5.1 fusion.18
  844.0 5.5 fusion.17
  849.4 5.1 fusion.16
  854.5 5.2 fusion.15
  860.7 2.3 collective-permute-start.4
  863.0 8.7 collective-permute-start.5
  871.7 2.8 collective-permute-done.4
  874.5 1.6 collective-permute-done.5
  876.2 2.1 collective-permute-start.6
  878.3 2.2 collective-permute-start.7
  880.6 2.9 collective-permute-done.7
  886.6 2.9 copy-done.9
  889.6 8.1 fusion.8
  897.6 1.2 fusion.248
  (320 shorter events, 46.7 us)
Async XLA Ops:
  7.2 882.4 %copy-start = (bf16[27,16]{0,1:T(8,128)(2,1)S(1)}, bf16[27,16]{0,1:T(8,128)(2,1)}, u32[]{:S(2)}) copy-start(bf16[27,16]{0,1:T(8,128)(2,1)} %param.13) | copy-start | bytes 2596
  7.2 737.0 %all-reduce.5.cloned.1.call-start = ((), (), s32[]{:S(2)}) async-start(), calls=%async_computation | async-start | bytes 1048576 | tf_op jit(solution)/shard_map/psum | solution.py:50
  8.3 8.3 collective-permute-start
  11.7 5.6 collective-permute-start.1
  17.4 0.7 copy-start.1
  39.0 9.3 %copy-start.2 = (bf16[94,2048]{1,0:T(8,128)(2,1)S(1)}, bf16[94,2048]{1,0:T(8,128)(2,1)}, u32[]{:S(2)}) copy-start(bf16[94,2048]{1,0:T(8,128)(2,1)} %copy-done.1) | copy-start | bytes 1155076
  92.0 6.5 copy-start.8
  92.0 652.2 %copy-start.4 = (f32[64,2048]{1,0:T(8,128)S(1)}, f32[64,2048]{1,0:T(8,128)}, u32[]{:S(2)}) copy-start(f32[64,2048]{1,0:T(8,128)} %param.11) | copy-start | bytes 1572868
  97.7 0.8 copy-start.5
  745.4 53.4 %collective-permute-start.2 = (bf16[15,2048]{1,0:T(8,128)(2,1)S(1)}, bf16[15,2048]{1,0:T(8,128)(2,1)S(1)}, u32[]{:S(2)}, u32[]{:S(2)}) collective-permute-start(bf16[15,2048]{1,0:T(8,128)(2,1)S(1)} %get-tuple-element.349), channel_id=1, source_target_pairs={{0,1},{1,2},{2,3},{4,5},{5,6},{6,7},{8,9},{9,10},{10,11},{12,13},{... | collective-permute-start | bytes 184328 | tf_op jit(solution)/shard_map/ppermute | solution.py:16
  796.8 5.6 collective-permute-start.3
  854.5 5.3 copy-start.3
  854.5 5.3 copy-start.6
  854.5 5.3 copy-start.7
  860.7 13.8 %collective-permute-start.4 = (bf16[1,64,2048]{2,1,0:T(8,128)(2,1)S(1)}, bf16[1,64,2048]{2,1,0:T(8,128)(2,1)S(1)}, u32[]{:S(2)}, u32[]{:S(2)}) collective-permute-start(bf16[1,64,2048]{2,1,0:T(8,128)(2,1)S(1)} %get-tuple-element.5), channel_id=1, source_target_pairs={{0,4},{4,8},{8,12},{12,16},{16,20},{20,24},{24,28},{28,32},{32,36}... | collective-permute-start | bytes 786440 | tf_op jit(solution)/shard_map/ppermute | solution.py:16
  863.0 13.1 %collective-permute-start.5 = (bf16[1,64,2048]{2,1,0:T(8,128)(2,1)S(1)}, bf16[1,64,2048]{2,1,0:T(8,128)(2,1)S(1)}, u32[]{:S(2)}, u32[]{:S(2)}) collective-permute-start(bf16[1,64,2048]{2,1,0:T(8,128)(2,1)S(1)} %get-tuple-element.5), channel_id=1, source_target_pairs={{4,0},{8,4},{12,8},{16,12},{20,16},{24,20},{28,24},{32,28},{36,32}... | collective-permute-start | bytes 786440 | tf_op jit(solution)/shard_map/ppermute | solution.py:19
  876.2 4.3 collective-permute-start.6
  878.3 5.1 collective-permute-start.7
  886.1 3.5 copy-start.10
  886.1 3.4 copy-start.11
  886.6 2.9 copy-start.9
Sparse Core Ops, SparseCore 0:
  98.6 645.5 all-reduce.4
where the time goes:
time: 916 us; the launch traced here: 906 us
  waiting for transfers between devices  656 us (72%)
  matrix products  96.7 us (11%)
  starting transfers between devices  71.8 us (8%)
  local copies, waits for them, and re-layouts  45 us (5%)
  other arithmetic  21.3 us (2%)
  between operations  15.5 us (2%)
    psum x1, waiting for transfers between devices, shards(): sensor = lax.psum(partial_value, 'depth')  646 us
    dot_general x16, matrix products, project(): jnp.dot(stacked, band_matrix, preferred_element_type=jnp.float32)  83.5 us
    ppermute x4, starting transfers between devices, padded_2(): lax.ppermute(lax.slice_in_dim(block, block.shape[dim] - width, None, axis...  57 us
    unnamed x164, local copies, waits for them, and re-layouts  44.4 us
  transfers between devices with their start and end apart: 9, of which 6 were waited for; matrix products, arithmetic and copies ran while one was open for 1% of the time, Pallas kernels for 0%

commit v1 on v0

--- a/solution.py
+++ b/solution.py
@@ -1,3 +1,4 @@
+import functools
 import jax
 import jax.numpy as jnp
 from jax import lax
@@ -6,6 +7,13 @@
 KS = 31
 step_size = 4.0
 penalty = 0.5
+
+
+def roots_pack(unit, mesh_dim):
+    return jnp.sum(lax.all_gather(unit, mesh_dim), axis=0)
+
+
+choose_the_vectors = functools.partial(roots_pack, mesh_dim="depth")
 
 
 def padded_2(block, sides, width):
@@ -47,7 +55,7 @@
     planes_half = planes.astype(jnp.bfloat16)
     rimmed = padded_2(planes_half, (("band", 1),), edge)
     partial_value = project(rimmed[0], lenslet_psf[0])
-    sensor = lax.psum(partial_value, "depth")
+    sensor = choose_the_vectors(partial_value)
     residual = (sensor - measured).astype(jnp.bfloat16)
     residual_rimmed = padded_2(residual, (("band", 0),), edge)
     gradient = jnp.stack([project(residual_rimmed, lenslet_psf[0][::-1, ::-1])])

time: 916 us -> 577 us (0.63)
  waiting for transfers between devices: 656 us -> 351 us
  starting transfers between devices: 71.8 us -> 27.3 us
  other arithmetic: 21.3 us -> 31.9 us
    psum x1 -> x0, waiting for transfers between devices: 646 us -> none  [shards(): sensor = lax.psum(partial_value, 'depth')]
    all_gather x0 -> x1, waiting for transfers between devices: none -> 341 us  [roots_pack(): return jnp.sum(lax.all_gather(unit, mesh_dim), axis=0)]
    ppermute x4, starting transfers between devices: 57 us -> 12.1 us  [padded_2(): lax.ppermute(lax.slice_in_dim(block, block.shape[dim] - width, None, axis...]
    reduce_sum x0 -> x1, other arithmetic: none -> 11.7 us  [roots_pack(): return jnp.sum(lax.all_gather(unit, mesh_dim), axis=0)]
where the time goes in v1:
time: 577 us; the launch traced here: 567 us
  waiting for transfers between devices  351 us (61%)
  matrix products  96.9 us (17%)
  local copies, waits for them, and re-layouts  45 us (8%)
  other arithmetic  31.9 us (6%)
  starting transfers between devices  27.3 us (5%)
  between operations  15.5 us (3%)
    all_gather x1, waiting for transfers between devices, roots_pack(): return jnp.sum(lax.all_gather(unit, mesh_dim), axis=0)  341 us
    dot_general x16, matrix products, project(): jnp.dot(stacked, band_matrix, preferred_element_type=jnp.float32)  83.7 us
    unnamed x164, local copies, waits for them, and re-layouts  44.4 us
    ppermute x4, starting transfers between devices, padded_2(): lax.ppermute(lax.slice_in_dim(block, 0, width, axis=dim), axis, backward)  15.2 us
    unnamed x144, other arithmetic  15 us
    ppermute x4, starting transfers between devices, padded_2(): lax.ppermute(lax.slice_in_dim(block, block.shape[dim] - width, None, axis...  12.1 us
    reduce_sum x1, other arithmetic, roots_pack(): return jnp.sum(lax.all_gather(unit, mesh_dim), axis=0)  11.7 us
  transfers between devices with their start and end apart: 9, of which 6 were waited for; matrix products, arithmetic and copies ran while one was open for 1% of the time, Pallas kernels for 0%

profile of v1, /device:TPU:5, one launch (start us, length us, event | category | flops | bytes accessed | tf_op | source)
XLA Modules:
  0.0 567.1 jit_solution(11259282851413785533)
XLA Ops:
  8.3 3.4 collective-permute-start
  11.7 1.9 collective-permute-start.1
  13.7 2.9 convert_bitcast_fusion.1
  19.3 1.2 constant_dynamic-update-slice_fusion.152
  20.5 1.2 constant_dynamic-update-slice_fusion.151
  21.6 1.2 constant_dynamic-update-slice_fusion.150
  22.8 1.2 constant_dynamic-update-slice_fusion.149
  24.0 1.2 constant_dynamic-update-slice_fusion.148
  25.1 1.2 constant_dynamic-update-slice_fusion.147
  27.4 1.2 constant_dynamic-update-slice_fusion.145
  28.6 1.2 constant_dynamic-update-slice_fusion.144
  29.7 1.2 constant_dynamic-update-slice_fusion.143
  30.9 1.2 constant_dynamic-update-slice_fusion.142
  32.1 1.2 constant_dynamic-update-slice_fusion.141
  39.0 1.2 constant_dynamic-update-slice_fusion.135
  43.7 1.2 constant_dynamic-update-slice_fusion.131
  55.7 5.2 fusion.30
  61.0 5.1 fusion.29
  66.0 5.3 fusion.28
  71.3 5.1 fusion.27
  76.3 5.5 fusion.26
  81.9 5.1 fusion.25
  86.9 5.1 fusion.24
  92.0 5.9 %fusion.23 = f32[64,2048]{1,0:T(8,128)S(1)} fusion(f32[64,2048]{1,0:T(8,128)S(1)} %fusion.24, bf16[64,31,286]{2,0,1:T(8,128)(2,1)S(1)} %get-tuple-element.72, bf16[31,286,256]{2,0,1:T(8,128)(2,1)S(1)} %convert_bitcast_fusion.1), kind=kOutput, calls=%fused_computation.212 | convolution fusion | flops 290521088 | bytes 6275072 | tf_op jit(solution)/shard_map/dot_general | solution.py:48
  98.8 340.6 %all-gather.3.cloned.1.call-done = f32[4096,2048]{1,0:T(8,128)} async-done(((f32[64,2048]{1,0:T(8,128)}), f32[4096,2048]{1,0:T(8,128)}) %all-gather.3.cloned.1.call-update) | async-done | bytes 33554448 | tf_op jit(solution)/shard_map/all_gather | solution.py:13
  439.4 11.7 %reduce_sum.9 = f32[64,2048]{1,0:T(8,128)S(1)} reduce(f32[64,64,2048]{2,1,0:T(8,128)} %bitcast.1719, f32[]{:T(128)} %constant.1.clone.1), dimensions={0}, to_apply=%region_0.1 | reduce | flops 8257536 | bytes 34078724 | tf_op jit(solution)/shard_map/reduce_sum | solution.py:13
  451.2 4.7 collective-permute-start.2
  455.8 2.2 convert_bitcast_fusion
  458.1 1.9 collective-permute-start.3
  461.8 1.9 collective-permute-done.3
  474.0 5.5 fusion.22
  484.8 5.0 fusion.21
  489.9 5.2 fusion.20
  495.1 5.1 fusion.19
  500.2 5.1 fusion.18
  505.2 5.5 fusion.17
  510.7 5.1 fusion.16
  515.8 5.2 fusion.15
  522.0 1.9 collective-permute-start.4
  523.9 9.1 %collective-permute-start.5 = (bf16[1,64,2048]{2,1,0:T(8,128)(2,1)S(1)}, bf16[1,64,2048]{2,1,0:T(8,128)(2,1)S(1)}, u32[]{:S(2)}, u32[]{:S(2)}) collective-permute-start(bf16[1,64,2048]{2,1,0:T(8,128)(2,1)S(1)} %get-tuple-element.5), channel_id=1, source_target_pairs={{4,0},{8,4},{12,8},{16,12},{20,16},{24,20},{28,24},{32,28},{36,32}... | collective-permute-start | bytes 786440 | tf_op jit(solution)/shard_map/ppermute | solution.py:27
  533.0 2.7 collective-permute-done.4
  535.7 1.8 collective-permute-done.5
  537.5 2.1 collective-permute-start.6
  539.6 2.2 collective-permute-start.7
  541.8 2.9 collective-permute-done.7
  547.9 2.9 copy-done.9
  550.8 8.1 %fusion.8 = f32[1,64,2048]{2,0,1:T(1,128)S(1)} fusion(bf16[27,64,2048]{2,1,0:T(8,128)(2,1)} %bitcast.1721, f32[16]{0:T(128)S(1)} %copy-done.10, bf16[27,16]{0,1:T(8,128)(2,1)S(1)} %copy-done, bf16[16]{0:T(256)(128)(2,1)S(1)} %copy-done.11), kind=kOutput, calls=%fused_computation.188 | convolution fusion | flops 123731968 | bytes 7603136 | tf_op jit(solution)/shard_map/n,nprc->prc/dot_general | solution.py:75
  558.9 1.2 fusion.248
  (321 shorter events, 46.8 us)
Async XLA Ops:
  7.2 543.6 %copy-start = (bf16[27,16]{0,1:T(8,128)(2,1)S(1)}, bf16[27,16]{0,1:T(8,128)(2,1)}, u32[]{:S(2)}) copy-start(bf16[27,16]{0,1:T(8,128)(2,1)} %param.13) | copy-start | bytes 2596
  7.2 432.2 %all-gather.3.cloned.1.call-start = ((), (), s32[]{:S(2)}) async-start(), calls=%async_computation | async-start | bytes 34078720 | tf_op jit(solution)/shard_map/all_gather | solution.py:13
  8.3 8.3 %collective-permute-start = (bf16[1,15,2048]{2,1,0:T(8,128)(2,1)S(1)}, bf16[1,15,2048]{2,1,0:T(8,128)(2,1)S(1)}, u32[]{:S(2)}, u32[]{:S(2)}) collective-permute-start(bf16[1,15,2048]{2,1,0:T(8,128)(2,1)S(1)} %get-tuple-element.351), channel_id=1, source_target_pairs={{0,1},{1,2},{2,3},{4,5},{5,6},{6,7},{8,9},{9,10},{10,11},{12,13},{... | collective-permute-start | bytes 184328 | tf_op jit(solution)/shard_map/ppermute | solution.py:24
  11.7 5.6 collective-permute-start.1
  17.4 0.7 copy-start.1
  39.0 9.3 %copy-start.2 = (bf16[94,2048]{1,0:T(8,128)(2,1)S(1)}, bf16[94,2048]{1,0:T(8,128)(2,1)}, u32[]{:S(2)}) copy-start(bf16[94,2048]{1,0:T(8,128)(2,1)} %copy-done.1) | copy-start | bytes 1155076
  92.0 6.7 %copy-start.8 = (bf16[1,31,31]{2,1,0:T(8,128)(2,1)S(1)}, bf16[1,31,31]{2,1,0:T(8,128)(2,1)}, u32[]{:S(2)}) copy-start(bf16[1,31,31]{2,1,0:T(8,128)(2,1)} %param.12) | copy-start | bytes 5770
  97.8 0.8 copy-start.5
  439.4 11.7 %copy-start.4 = (f32[64,2048]{1,0:T(8,128)S(1)}, f32[64,2048]{1,0:T(8,128)}, u32[]{:S(2)}) copy-start(f32[64,2048]{1,0:T(8,128)} %param.11) | copy-start | bytes 1572868
  451.2 8.8 %collective-permute-start.2 = (bf16[15,2048]{1,0:T(8,128)(2,1)S(1)}, bf16[15,2048]{1,0:T(8,128)(2,1)S(1)}, u32[]{:S(2)}, u32[]{:S(2)}) collective-permute-start(bf16[15,2048]{1,0:T(8,128)(2,1)S(1)} %get-tuple-element.349), channel_id=1, source_target_pairs={{0,1},{1,2},{2,3},{4,5},{5,6},{6,7},{8,9},{9,10},{10,11},{12,13},{... | collective-permute-start | bytes 184328 | tf_op jit(solution)/shard_map/ppermute | solution.py:24
  458.1 5.6 collective-permute-start.3
  515.7 5.3 copy-start.3
  515.7 5.3 copy-start.6
  515.7 5.3 copy-start.7
  522.0 13.7 %collective-permute-start.4 = (bf16[1,64,2048]{2,1,0:T(8,128)(2,1)S(1)}, bf16[1,64,2048]{2,1,0:T(8,128)(2,1)S(1)}, u32[]{:S(2)}, u32[]{:S(2)}) collective-permute-start(bf16[1,64,2048]{2,1,0:T(8,128)(2,1)S(1)} %get-tuple-element.5), channel_id=1, source_target_pairs={{0,4},{4,8},{8,12},{12,16},{16,20},{20,24},{24,28},{28,32},{32,36}... | collective-permute-start | bytes 786440 | tf_op jit(solution)/shard_map/ppermute | solution.py:24
  523.9 13.5 %collective-permute-start.5 = (bf16[1,64,2048]{2,1,0:T(8,128)(2,1)S(1)}, bf16[1,64,2048]{2,1,0:T(8,128)(2,1)S(1)}, u32[]{:S(2)}, u32[]{:S(2)}) collective-permute-start(bf16[1,64,2048]{2,1,0:T(8,128)(2,1)S(1)} %get-tuple-element.5), channel_id=1, source_target_pairs={{4,0},{8,4},{12,8},{16,12},{20,16},{24,20},{28,24},{32,28},{36,32}... | collective-permute-start | bytes 786440 | tf_op jit(solution)/shard_map/ppermute | solution.py:27
  537.5 4.3 collective-permute-start.6
  539.6 5.1 collective-permute-start.7
  547.3 3.5 copy-start.10
  547.4 3.4 copy-start.11
  547.9 2.9 copy-start.9
Sparse Core Ops, SparseCore 0:
  98.8 340.5 all-gather.2
